TPU v7x, 512 devices: a whole 4x4x16 slice. The times are simulated.
512 devices in a mesh: dp: 16 (over z), axial: 32 (over x, y, core).
Axes of the slice: x: 4, y: 4, z: 16, core: 2. Of those that a mesh axis runs over, the one named last changes fastest.
Arguments:
- pair: bfloat16 [16, 256, 256, 128], P('dp', 'axial'), may hold values from -6 to 6
- cotangent: bfloat16 [16, 256, 256, 128], P('dp', 'axial'), may hold values from -6 to 6
- lengths: int32 [16], P('dp'), may hold values from 1 to 256, 2560 in all
- outgo_norm: float32 [128], replicated, may hold values from 0.1 to 1.9
- outgo_proj: float32 [128, 640], replicated, may hold values from -0.5 to 0.5
- outgo_gain: float32 [128], replicated, may hold values from 0.1 to 1.9
- outgo_final: float32 [128, 128], replicated, may hold values from -0.5 to 0.5
- incom_norm: float32 [128], replicated, may hold values from 0.1 to 1.9
- incom_proj: float32 [128, 640], replicated, may hold values from -0.5 to 0.5
- incom_gain: float32 [128], replicated, may hold values from 0.1 to 1.9
- incom_final: float32 [128, 128], replicated, may hold values from -0.5 to 0.5
Outputs:
- grad_pair: float32 [16, 256, 256, 128], P('dp', 'axial')
- grad_outgo_norm: float32 [128], replicated
- grad_outgo_proj: float32 [128, 640], replicated
- grad_outgo_gain: float32 [128], replicated
- grad_outgo_final: float32 [128, 128], replicated
- grad_incom_norm: float32 [128], replicated
- grad_incom_proj: float32 [128, 640], replicated
- grad_incom_gain: float32 [128], replicated
- grad_incom_final: float32 [128, 128], replicated
Inputs may be any that keep to these rules, and one draw needn't show every extreme that they name: lengths[c] is the crop length of complex c; some complex has exactly 256 tokens.
All inputs are finite; a program needn't handle non-finite values. No bound on the sum of `lengths` on one device may be relied on, other than what follows from the above.
Results may differ from a plain program's by a relative error of at most 0.03.
Values may be sent and summed in bfloat16 or wider, within the bound.
A program may use at most 128 MiB of HBM per device.

v0:
```python
import math

import jax
import jax.numpy as jnp
from jax import lax
from jax.sharding import PartitionSpec as P

EPSILON = 1e-05


def rounded(inputs):
    return lax.optimization_barrier(inputs.astype(jnp.bfloat16)).astype(jnp.float32)


def layer_norm(inputs, factor):
    average = jnp.mean(inputs, axis=-1, keepdims=True)
    centered = inputs - average
    spread = jnp.mean(centered * centered, axis=-1, keepdims=True)
    return centered * lax.rsqrt(spread + EPSILON) * factor


def gating(mixture, pair_mask, hidden):
    left_part = (
        mixture[:, :hidden] * jax.nn.sigmoid(mixture[:, 2 * hidden : 3 * hidden]) * pair_mask
    )
    right_part = (
        mixture[:, hidden : 2 * hidden]
        * jax.nn.sigmoid(mixture[:, 3 * hidden : 4 * hidden])
        * pair_mask
    )
    gate_part = jax.nn.sigmoid(mixture[:, 4 * hidden :])
    return (left_part, right_part, gate_part)


def entry(flat_pair, norm_gain, projection, pair_mask, hidden):
    normed = layer_norm(flat_pair, norm_gain).astype(jnp.bfloat16)
    mixture = jnp.dot(normed, projection.astype(jnp.bfloat16), preferred_element_type=jnp.float32)
    left_part, right_part, gate_part = gating(mixture, pair_mask, hidden)
    return (normed, mixture, left_part, right_part, gate_part)


def entry_back(
    flat_pair,
    norm_gain,
    projection,
    pair_mask,
    hidden,
    normed,
    mixture,
    grad_left,
    grad_right,
    grad_gate,
):
    unused, pull_gate = jax.vjp(lambda inner_mix: gating(inner_mix, pair_mask, hidden), mixture)
    grad_mixture = pull_gate((grad_left, grad_right, grad_gate))[0].astype(jnp.bfloat16)
    grad_projection = jnp.dot(normed.T, grad_mixture, preferred_element_type=jnp.float32)
    grad_normed = jnp.dot(
        grad_mixture, projection.astype(jnp.bfloat16).T, preferred_element_type=jnp.float32
    )
    unused, pull_norm = jax.vjp(layer_norm, flat_pair, norm_gain)
    grad_flat, grad_gain = pull_norm(grad_normed)
    return (grad_flat, grad_gain, grad_projection)


def leave(inner_sum, gate_part, out_gain, final_weight):
    final_normed = layer_norm(inner_sum, out_gain).astype(jnp.bfloat16)
    product = jnp.dot(
        final_normed, final_weight.astype(jnp.bfloat16), preferred_element_type=jnp.float32
    )
    return (final_normed, product, product * gate_part)


def leave_back(inner_sum, gate_part, out_gain, final_weight, final_normed, product, grad_update):
    grad_product = (grad_update * gate_part).astype(jnp.bfloat16)
    grad_gate = grad_update * product
    grad_final = jnp.dot(final_normed.T, grad_product, preferred_element_type=jnp.float32)
    grad_normed = jnp.dot(
        grad_product, final_weight.astype(jnp.bfloat16).T, preferred_element_type=jnp.float32
    )
    unused, pull_norm = jax.vjp(layer_norm, inner_sum, out_gain)
    grad_inner, grad_gain = pull_norm(grad_normed)
    return (grad_inner, grad_gate, grad_gain, grad_final)


def channel_major(field, row_count, tokens):
    hidden = field.shape[1]
    return jnp.transpose(field.reshape(row_count, tokens, hidden), (2, 0, 1))


def row_major(field):
    hidden = field.shape[0]
    return jnp.transpose(field, (1, 2, 0)).reshape(-1, hidden)


def body(
    pair,
    cotangent,
    lengths,
    outgo_norm,
    outgo_proj,
    outgo_gain,
    outgo_final,
    incom_norm,
    incom_proj,
    incom_gain,
    incom_final,
):
    row_count = pair.shape[1]
    tokens = pair.shape[2]
    channels = pair.shape[3]
    hidden = outgo_gain.shape[0]
    length = lengths[0]
    first_row = lax.axis_index("axial") * row_count
    row_alive = (first_row + jnp.arange(row_count, dtype=jnp.int32) < length).astype(jnp.float32)
    column_alive = (jnp.arange(tokens, dtype=jnp.int32) < length).astype(jnp.float32)
    pair_mask = (row_alive[:, None] * column_alive[None, :]).reshape(-1, 1)
    flat_start = pair[0].reshape(-1, channels).astype(jnp.float32)
    normed_one, mixture_one, left_one, right_one, gate_one = entry(
        flat_start, outgo_norm, outgo_proj, pair_mask, hidden
    )
    left_first = channel_major(left_one.astype(jnp.bfloat16), row_count, tokens)
    right_first = channel_major(right_one.astype(jnp.bfloat16), row_count, tokens)
    left_owned, right_owned = (
        lax.all_to_all(left_first, "axial", split_axis=0, concat_axis=1, tiled=True),
        lax.all_to_all(right_first, "axial", split_axis=0, concat_axis=1, tiled=True),
    )
    inner_cols = jnp.einsum(
        "hik,hjk->hij", left_owned, right_owned, preferred_element_type=jnp.float32
    )
    inner_one = row_major(
        lax.all_to_all(
            inner_cols.astype(jnp.bfloat16), "axial", split_axis=1, concat_axis=0, tiled=True
        ).astype(inner_cols.dtype)
    )
    final_one, product_one, update_one = leave(inner_one, gate_one, outgo_gain, outgo_final)
    flat_middle = rounded(flat_start + update_one)
    normed_two, mixture_two, left_two, right_two, gate_two = entry(
        flat_middle, incom_norm, incom_proj, pair_mask, hidden
    )
    left_second = channel_major(left_two.astype(jnp.bfloat16), row_count, tokens)
    right_second = channel_major(right_two.astype(jnp.bfloat16), row_count, tokens)
    left_held, right_held = (
        lax.all_to_all(left_second, "axial", split_axis=0, concat_axis=1, tiled=True),
        lax.all_to_all(right_second, "axial", split_axis=0, concat_axis=1, tiled=True),
    )
    inner_held = jnp.einsum(
        "hki,hkj->hij", left_held, right_held, preferred_element_type=jnp.float32
    )
    inner_two = row_major(
        lax.all_to_all(
            inner_held.astype(jnp.bfloat16), "axial", split_axis=1, concat_axis=0, tiled=True
        ).astype(inner_held.dtype)
    )
    final_two, product_two, update_two = leave(inner_two, gate_two, incom_gain, incom_final)
    grad_end = cotangent[0].reshape(-1, channels).astype(jnp.float32)
    grad_inner_two, grad_gate_two, grad_gain_two, grad_final_two = leave_back(
        inner_two, gate_two, incom_gain, incom_final, final_two, product_two, grad_end
    )
    grad_cells_two = channel_major(grad_inner_two.astype(jnp.bfloat16), row_count, tokens)
    grad_held_two = lax.all_to_all(grad_cells_two, "axial", split_axis=0, concat_axis=1, tiled=True)
    left_back, right_back = (
        lax.all_to_all(left_second, "axial", split_axis=0, concat_axis=1, tiled=True),
        lax.all_to_all(right_second, "axial", split_axis=0, concat_axis=1, tiled=True),
    )
    grad_left_held = jnp.einsum(
        "hij,hkj->hki", grad_held_two, right_back, preferred_element_type=jnp.float32
    )
    grad_right_held = jnp.einsum(
        "hki,hij->hkj", left_back, grad_held_two, preferred_element_type=jnp.float32
    )
    grad_left_rows, grad_right_rows = (
        lax.all_to_all(
            grad_left_held.astype(jnp.bfloat16), "axial", split_axis=1, concat_axis=0, tiled=True
        ).astype(grad_left_held.dtype),
        lax.all_to_all(
            grad_right_held.astype(jnp.bfloat16), "axial", split_axis=1, concat_axis=0, tiled=True
        ).astype(grad_right_held.dtype),
    )
    grad_left_two = row_major(grad_left_rows)
    grad_right_two = row_major(grad_right_rows)
    grad_flat_two, grad_norm_two, grad_proj_two = entry_back(
        flat_middle,
        incom_norm,
        incom_proj,
        pair_mask,
        hidden,
        normed_two,
        mixture_two,
        grad_left_two,
        grad_right_two,
        grad_gate_two,
    )
    second_sums = lax.psum(
        (grad_norm_two, grad_proj_two, grad_gain_two, grad_final_two), ("dp", "axial")
    )
    grad_middle = grad_end + grad_flat_two
    grad_inner_one, grad_gate_one, grad_gain_one, grad_final_one = leave_back(
        inner_one, gate_one, outgo_gain, outgo_final, final_one, product_one, grad_middle
    )
    grad_cells_one = channel_major(grad_inner_one.astype(jnp.bfloat16), row_count, tokens)
    grad_owned_one = lax.all_to_all(
        grad_cells_one, "axial", split_axis=0, concat_axis=1, tiled=True
    )
    left_again, right_again = (
        lax.all_to_all(left_first, "axial", split_axis=0, concat_axis=1, tiled=True),
        lax.all_to_all(right_first, "axial", split_axis=0, concat_axis=1, tiled=True),
    )
    grad_left_owned = jnp.einsum(
        "hij,hjk->hik", grad_owned_one, right_again, preferred_element_type=jnp.float32
    )
    grad_right_owned = jnp.einsum(
        "hij,hik->hjk", grad_owned_one, left_again, preferred_element_type=jnp.float32
    )
    grad_left_back, grad_right_back = (
        lax.all_to_all(
            grad_left_owned.astype(jnp.bfloat16), "axial", split_axis=1, concat_axis=0, tiled=True
        ).astype(grad_left_owned.dtype),
        lax.all_to_all(
            grad_right_owned.astype(jnp.bfloat16), "axial", split_axis=1, concat_axis=0, tiled=True
        ).astype(grad_right_owned.dtype),
    )
    grad_left_one = row_major(grad_left_back)
    grad_right_one = row_major(grad_right_back)
    grad_flat_one, grad_norm_one, grad_proj_one = entry_back(
        flat_start,
        outgo_norm,
        outgo_proj,
        pair_mask,
        hidden,
        normed_one,
        mixture_one,
        grad_left_one,
        grad_right_one,
        grad_gate_one,
    )
    grad_begin = grad_middle + grad_flat_one
    first_sums = lax.psum(
        (grad_norm_one, grad_proj_one, grad_gain_one, grad_final_one), ("dp", "axial")
    )
    totals = tuple(first_sums) + tuple(second_sums)
    scale = 1.0 / math.sqrt(lax.axis_size("dp") * tokens * tokens)
    return (
        grad_begin.reshape(1, row_count, tokens, channels),
        totals[0] * scale,
        totals[1] * scale,
        totals[2] * scale,
        totals[3] * scale,
        totals[4] * scale,
        totals[5] * scale,
        totals[6] * scale,
        totals[7] * scale,
    )


def solution(mesh):
    return jax.shard_map(
        body,
        mesh=mesh,
        in_specs=(
            P("dp", "axial", None, None),
            P("dp", "axial", None, None),
            P("dp"),
            P(),
            P(),
            P(),
            P(),
            P(),
            P(),
            P(),
            P(),
        ),
        out_specs=(P("dp", "axial", None, None), P(), P(), P(), P(), P(), P(), P(), P()),
        check_vma=False,
    )
```

profile of v0, /device:TPU:1, one launch (start us, length us, event | category | flops | bytes accessed | tf_op | source)
XLA Modules:
  0.0 852.8 jit_solution(13527251584811730097)
XLA Ops:
  7.2 1.3 convert_reduce_fusion.1
  8.5 1.7 fusion.44
  10.9 1.6 fusion.40
  12.6 2.0 fusion.80
  14.6 2.3 copy-done
  17.5 1.2 copy.86
  18.7 10.4 %all-to-all-start.1 = ((bf16[128,8,256]{2,1,0:T(8,128)(2,1)}), bf16[128,8,256]{2,1,0:T(8,128)(2,1)S(1)}, u32[]{:S(2)}, u32[]{:S(2)}) async-start(bf16[128,8,256]{2,1,0:T(8,128)(2,1)} %bitcast.10), calls=%async_computation.1 | async-start | bytes 1048576 | tf_op jit(solution)/shard_map/all_to_all | solution.py:125
  29.5 11.3 %all-to-all-done.1 = bf16[128,8,256]{2,1,0:T(8,128)(2,1)S(1)} async-done(((bf16[128,8,256]{2,1,0:T(8,128)(2,1)}), bf16[128,8,256]{2,1,0:T(8,128)(2,1)S(1)}, u32[]{:S(2)}, u32[]{:S(2)}) %all-to-all-start.1) | async-done | bytes 524320 | tf_op jit(solution)/shard_map/all_to_all | solution.py:125
  40.8 15.0 %all_to_all.182 = bf16[128,8,256]{2,1,0:T(8,128)(2,1)S(1)} all-to-all(bf16[128,8,256]{2,1,0:T(8,128)(2,1)S(1)} %bitcast.257), channel_id=1, replica_groups=mesh['dp'=16,'axial'=32] {'axial'}, dimensions={0} | all-to-all | bytes 1048576 | tf_op jit(solution)/shard_map/all_to_all | solution.py:124
  57.1 15.2 %all_to_all.183 = bf16[4,256,256]{2,0,1:T(4,128)(2,1)S(1)} all-to-all(bf16[4,256,256]{2,0,1:T(4,128)(2,1)S(1)} %copy.88), channel_id=1, replica_groups=mesh['dp'=16,'axial'=32] {'axial'}, dimensions={1} | all-to-all | bytes 1048576 | tf_op jit(solution)/shard_map/all_to_all | solution.py:131
  73.9 2.8 fusion.45
  78.6 2.3 copy-done.1
  80.9 1.7 multiply_convert_fusion.3
  83.8 3.7 all-to-all-start.4
  87.5 1.2 copy.92
  88.7 10.4 %all-to-all-done.4 = bf16[128,8,256]{2,1,0:T(8,128)(2,1)S(1)} async-done(((bf16[128,8,256]{2,1,0:T(8,128)(2,1)}), bf16[128,8,256]{2,1,0:T(8,128)(2,1)S(1)}, u32[]{:S(2)}, u32[]{:S(2)}) %all-to-all-start.4) | async-done | bytes 524320 | tf_op jit(solution)/shard_map/all_to_all | solution.py:144
  99.1 15.2 %all_to_all.184 = bf16[128,8,256]{2,1,0:T(8,128)(2,1)S(1)} all-to-all(bf16[128,8,256]{2,1,0:T(8,128)(2,1)} %bitcast.258), channel_id=1, replica_groups=mesh['dp'=16,'axial'=32] {'axial'}, dimensions={0} | all-to-all | bytes 1048576 | tf_op jit(solution)/shard_map/all_to_all | solution.py:143
  115.1 15.0 %all_to_all.185 = bf16[4,256,256]{2,0,1:T(4,128)(2,1)S(1)} all-to-all(bf16[4,256,256]{2,0,1:T(4,128)(2,1)S(1)} %copy.97), channel_id=1, replica_groups=mesh['dp'=16,'axial'=32] {'axial'}, dimensions={1} | all-to-all | bytes 1048576 | tf_op jit(solution)/shard_map/all_to_all | solution.py:150
  131.1 1.4 copy.100
  133.4 2.8 multiply_reduce_fusion
  136.3 3.0 fusion.99
  140.4 2.2 copy.101
  142.6 15.2 %all_to_all.186 = bf16[128,8,256]{2,1,0:T(8,128)(2,1)S(1)} all-to-all(bf16[128,8,256]{2,1,0:T(8,128)(2,1)} %bitcast.259), channel_id=1, replica_groups=mesh['dp'=16,'axial'=32] {'axial'}, dimensions={0} | all-to-all | bytes 1048576 | tf_op jit(solution)/shard_map/all_to_all | solution.py:160
  158.7 1.3 convolution_convert_fusion.3
  160.1 1.2 copy.103
  161.3 4.4 all-to-all-start.7
  165.7 1.4 convolution_convert_fusion.2
  167.1 1.2 copy.107
  168.3 8.8 %all-to-all-done.7 = bf16[4,256,256]{2,0,1:T(4,128)(2,1)} async-done(((bf16[4,256,256]{2,0,1:T(4,128)(2,1)}), bf16[4,256,256]{2,0,1:T(4,128)(2,1)}, u32[]{:S(2)}, u32[]{:S(2)}) %all-to-all-start.7) | async-done | bytes 524320 | tf_op jit(solution)/shard_map/all_to_all | solution.py:175
  177.1 4.6 all-to-all-start.8
  181.7 2.8 fusion
  186.8 1.6 copy.106
  188.4 4.5 all-to-all-done.8
  195.2 2.6 copy.110
  197.8 3.0 fusion.11
  201.2 1.5 copy-done.3
  202.7 1.5 fusion.8
  204.2 1.3 fusion.98
  205.5 2.7 fusion.13
  209.2 1.4 fusion.97
  211.0 1.2 copy.111
  212.2 3.7 all-to-all-start.9
  215.9 2.2 fusion.102
  218.1 9.4 %all-to-all-done.9 = bf16[128,8,256]{2,1,0:T(8,128)(2,1)S(1)} async-done(((bf16[128,8,256]{2,1,0:T(8,128)(2,1)}), bf16[128,8,256]{2,1,0:T(8,128)(2,1)S(1)}, u32[]{:S(2)}, u32[]{:S(2)}) %all-to-all-start.9) | async-done | bytes 524320 | tf_op jit(solution)/shard_map/all_to_all | solution.py:201
  227.4 1.6 convolution_convert_fusion.1
  229.0 1.3 copy.114
  230.3 3.7 all-to-all-start.10
  234.0 3.7 fusion.93
  237.7 1.5 convolution_convert_fusion
  239.2 1.2 copy.118
  240.4 5.1 all-to-all-done.10
  245.6 4.4 all-to-all-start.11
  250.3 2.0 fusion.101
  253.5 1.6 copy.117
  255.1 6.2 all-to-all-done.11
  263.6 2.6 copy.121
  266.2 3.0 fusion.14
  271.2 1.3 fusion.100
  272.5 1.3 fusion.41
  273.8 105.2 %all-reduce.10 = (f32[128]{0:T(128)S(1)}, f32[128]{0:T(128)S(1)}, f32[128]{0:T(128)S(1)}, f32[128]{0:T(128)S(1)}) all-reduce(f32[128]{0:T(128)S(1)} %get-tuple-element.13, f32[128]{0:T(128)S(1)} %get-tuple-element.11, f32[128]{0:T(128)S(1)} %copy-done.33, f32[128]{0:T(128)S(1)} %copy-done.32), channel_id=1, replica_groups=mesh['dp'=16,'axial'=32] {'dp','axial'}, use_global_device_ids=true, to_apply=%region_17.0 | all-reduce | flops 512 | bytes 4096 | tf_op jit(solution)/shard_map/psum | solution.py:237
  380.1 2.8 add_add_fusion.4
  383.0 459.5 %all-reduce.14.cloned.1.call-done = (f32[128,640]{1,0:T(8,128)}, f32[128,128]{1,0:T(8,128)}, f32[128,640]{1,0:T(8,128)}, f32[128,128]{1,0:T(8,128)}) async-done(((f32[128,640]{1,0:T(8,128)}, f32[128,128]{1,0:T(8,128)}, f32[128,640]{1,0:T(8,128)}, f32[128,128]{1,0:T(8,128)}), (f32[128,640]{1,0:T(8,128)}, f32[128,128]{1,0:T(8,128)}, f32[128,640]{1,0:T(8,128)}, ...) | async-done | bytes 786448 | tf_op jit(solution)/shard_map/psum | solution.py:237
  842.4 1.9 broadcast_multiply_fusion
  844.4 1.5 broadcast_multiply_fusion.2
  (132 shorter events, 24.5 us)
Async XLA Ops:
  12.6 4.9 copy-start.10
  14.6 2.3 copy-start
  18.7 22.2 %all-to-all-start.1 = ((bf16[128,8,256]{2,1,0:T(8,128)(2,1)}), bf16[128,8,256]{2,1,0:T(8,128)(2,1)S(1)}, u32[]{:S(2)}, u32[]{:S(2)}) async-start(bf16[128,8,256]{2,1,0:T(8,128)(2,1)} %bitcast.10), calls=%async_computation.1 | async-start | bytes 1048576 | tf_op jit(solution)/shard_map/all_to_all | solution.py:125
  40.8 31.8 %copy-start.22 = (bf16[128,8,256]{2,1,0:T(8,128)(2,1)}, bf16[128,8,256]{2,1,0:T(8,128)(2,1)S(1)}, u32[]{:S(2)}) copy-start(bf16[128,8,256]{2,1,0:T(8,128)(2,1)S(1)} %all-to-all-done.1) | copy-start | bytes 1572868
  55.8 0.8 copy-start.13
  56.6 16.6 %copy-start.30 = (f32[128]{0:T(128)S(1)}, f32[128]{0:T(128)}, u32[]{:S(2)}) copy-start(f32[128]{0:T(128)} %param.16) | copy-start | bytes 1540
  57.0 16.8 %copy-start.2 = (bf16[1,8,256,128]{3,2,1,0:T(8,128)(2,1)S(1)}, bf16[1,8,256,128]{3,2,1,0:T(8,128)(2,1)}, u32[]{:S(2)}) copy-start(bf16[1,8,256,128]{3,2,1,0:T(8,128)(2,1)} %param.11) | copy-start | bytes 1572868
  73.0 4.5 copy-start.24
  73.0 4.5 copy-start.27
  73.9 3.6 copy-start.18
  73.9 7.0 copy-start.4
  78.6 2.3 copy-start.1
  83.8 15.3 %all-to-all-start.4 = ((bf16[128,8,256]{2,1,0:T(8,128)(2,1)}), bf16[128,8,256]{2,1,0:T(8,128)(2,1)S(1)}, u32[]{:S(2)}, u32[]{:S(2)}) async-start(bf16[128,8,256]{2,1,0:T(8,128)(2,1)} %bitcast.256), calls=%async_computation.4 | async-start | bytes 1048576 | tf_op jit(solution)/shard_map/all_to_all | solution.py:144
  99.1 31.1 %copy-start.14 = (bf16[128,8,256]{2,1,0:T(8,128)(2,1)}, bf16[128,8,256]{2,1,0:T(8,128)(2,1)S(1)}, u32[]{:S(2)}) copy-start(bf16[128,8,256]{2,1,0:T(8,128)(2,1)S(1)} %all-to-all-done.4) | copy-start | bytes 1572868
  114.3 0.8 copy-start.16
  136.3 29.4 %copy-start.15 = (bf16[128,8,256]{2,1,0:T(8,128)(2,1)S(1)}, bf16[128,8,256]{2,1,0:T(8,128)(2,1)}, u32[]{:S(2)}) copy-start(bf16[128,8,256]{2,1,0:T(8,128)(2,1)} %copy-done.14) | copy-start | bytes 1572868
  139.3 42.4 %copy-start.5 = (bf16[1,8,256,128]{3,2,1,0:T(8,128)(2,1)S(1)}, bf16[1,8,256,128]{3,2,1,0:T(8,128)(2,1)}, u32[]{:S(2)}) copy-start(bf16[1,8,256,128]{3,2,1,0:T(8,128)(2,1)} %param.12) | copy-start | bytes 1572868
  157.9 0.8 copy-start.23
  161.3 15.8 %all-to-all-start.7 = ((bf16[4,256,256]{2,0,1:T(4,128)(2,1)}), bf16[4,256,256]{2,0,1:T(4,128)(2,1)}, u32[]{:S(2)}, u32[]{:S(2)}) async-start(bf16[4,256,256]{2,0,1:T(4,128)(2,1)} %copy.103), calls=%async_computation.7 | async-start | bytes 1048576 | tf_op jit(solution)/shard_map/all_to_all | solution.py:175
  177.1 15.8 %all-to-all-start.8 = ((bf16[4,256,256]{2,0,1:T(4,128)(2,1)}), bf16[4,256,256]{2,0,1:T(4,128)(2,1)}, u32[]{:S(2)}, u32[]{:S(2)}) async-start(bf16[4,256,256]{2,0,1:T(4,128)(2,1)} %copy.107), calls=%async_computation.8 | async-start | bytes 1048576 | tf_op jit(solution)/shard_map/all_to_all | solution.py:172
  197.8 3.0 copy-start.21
  200.8 1.8 copy-start.28
  201.1 1.5 copy-start.3
  202.6 2.9 copy-start.6
  202.6 2.9 copy-start.20
  202.6 5.6 copy-start.25
  202.6 5.6 copy-start.31
  208.3 2.3 copy-start.8
  209.2 24.8 %copy-start.29 = (f32[128]{0:T(128)S(1)}, f32[128]{0:T(128)}, u32[]{:S(2)}) copy-start(f32[128]{0:T(128)} %param.18) | copy-start | bytes 1540
  212.2 15.2 %all-to-all-start.9 = ((bf16[128,8,256]{2,1,0:T(8,128)(2,1)}), bf16[128,8,256]{2,1,0:T(8,128)(2,1)S(1)}, u32[]{:S(2)}, u32[]{:S(2)}) async-start(bf16[128,8,256]{2,1,0:T(8,128)(2,1)} %bitcast.255), calls=%async_computation.9 | async-start | bytes 1048576 | tf_op jit(solution)/shard_map/all_to_all | solution.py:201
  227.4 2.9 copy-start.17
  227.4 22.9 %copy-start.9 = (bf16[2048,128]{1,0:T(8,128)(2,1)S(1)}, bf16[2048,128]{1,0:T(8,128)(2,1)}, u32[]{:S(2)}) copy-start(bf16[2048,128]{1,0:T(8,128)(2,1)} %copy-done.8) | copy-start | bytes 1572868
  230.3 15.3 %all-to-all-start.10 = ((bf16[4,256,256]{2,0,1:T(4,128)(2,1)}), bf16[4,256,256]{2,0,1:T(4,128)(2,1)S(1)}, u32[]{:S(2)}, u32[]{:S(2)}) async-start(bf16[4,256,256]{2,0,1:T(4,128)(2,1)} %copy.114), calls=%async_computation.10 | async-start | bytes 1048576 | tf_op jit(solution)/shard_map/all_to_all | solution.py:218
  245.6 15.8 %all-to-all-start.11 = ((bf16[4,256,256]{2,0,1:T(4,128)(2,1)}), bf16[4,256,256]{2,0,1:T(4,128)(2,1)}, u32[]{:S(2)}, u32[]{:S(2)}) async-start(bf16[4,256,256]{2,0,1:T(4,128)(2,1)} %copy.118), calls=%async_computation.11 | async-start | bytes 1048576 | tf_op jit(solution)/shard_map/all_to_all | solution.py:215
  250.0 592.5 %all-reduce.14.cloned.1.call-start = ((), (), s32[]{:S(2)}) async-start(), calls=%async_computation.12 | async-start | bytes 1572864 | tf_op jit(solution)/shard_map/psum | solution.py:237
  266.2 3.1 copy-start.12
  269.2 1.0 copy-start.19
  269.2 1.0 copy-start.26
  269.2 1.9 copy-start.11
  270.2 3.6 copy-start.32
  270.2 3.6 copy-start.33
  270.2 109.9 %copy-start.7 = (bf16[1,8,256,128]{3,2,1,0:T(8,128)(2,1)S(1)}, bf16[1,8,256,128]{3,2,1,0:T(8,128)(2,1)}, u32[]{:S(2)}) copy-start(bf16[1,8,256,128]{3,2,1,0:T(8,128)(2,1)} %param.12) | copy-start | bytes 1572868
Sparse Core Ops, SparseCore 0:
  380.2 462.1 all-reduce.13
where the time goes:
time: 855 us; the launch traced here: 853 us
  waiting for transfers between devices  515 us (60%)
  blocking collectives  181 us (21%)
  other arithmetic  39.2 us (5%)
  local copies, waits for them, and re-layouts  36.3 us (4%)
  starting transfers between devices  35.2 us (4%)
  matrix products  30.6 us (4%)
  between operations  15.4 us (2%)
    psum x1, waiting for transfers between devices, body(): lax.psum((grad_norm_one, grad_proj_one, grad_gain_one, grad_final_one), (...  459 us
    psum x1, blocking collectives, body(): lax.psum((grad_norm_one, grad_proj_one, grad_gain_one, grad_final_one), (...  105 us
  transfers between devices with their start and end apart: 8, of which 8 were waited for; matrix products, arithmetic and copies ran while one was open for 3% of the time, Pallas kernels for 0%

commit v1 on v0

v1 whole, which is shorter than its diff:
```python
import functools
import math

import jax
import jax.numpy as jnp
from jax import lax
from jax.experimental import pallas as pl
from jax.experimental.pallas import tpu as pltpu
from jax.sharding import PartitionSpec as P

EPSILON = 1e-05
MESH = pl.DeviceIdType.MESH
F32, BF16 = jnp.float32, jnp.bfloat16
PARTS = 32
DEPTH = 16
ROWS, TOK, C = 8, 256, 128
CHUNKS = 2
W = TOK // CHUNKS
BLOCKS = ROWS * CHUNKS
CELLS = ROWS * TOK
PIECE, LANES = 16, 384


def dot(a, b, ca=1, cb=0):
    return lax.dot_general(a, b, (((ca,), (cb,)), ((), ())), preferred_element_type=F32)


def sigmoid(v):
    return 0.5 * jnp.tanh(0.5 * v) + 0.5


def center(v):
    c = v - jnp.mean(v, axis=0, keepdims=True)
    rs = lax.rsqrt(jnp.mean(c * c, axis=0, keepdims=True) + EPSILON)
    return c * rs, rs


def center_back(grad, hat, rs):
    return rs * (
        grad
        - jnp.mean(grad, axis=0, keepdims=True)
        - hat * jnp.mean(grad * hat, axis=0, keepdims=True)
    )


def partner(me, s):
    u = s + s // 20
    dx, dy, dc = (2 + 3 * (u // 8)) % 4, (2 + 3 * ((u // 2) % 4)) % 4, u % 2
    x, y, c = me // 8, (me // 2) % 4, me % 2
    return ((x + dx) % 4) * 8 + ((y + dy) % 4) * 2 + (c + dc) % 2


def kernel(
    len_ref, pair_ref, cot_ref, n1_ref, p1_ref, g1_ref, f1_ref, n2_ref, p2_ref, g2_ref, f2_ref,
    out_ref, on1, op1, og1, of1, on2, op2, og2, of2,
    gnb, ggb, pjt, pj, fnt, fw, xt, ct, xh, rsx, st, nrm, gm, fnn, gp, ih, rsi, prod, acc_n, acc_g,
    tmp, sa, ra, sb, rb, tri, ws, wr, zs, zr, cs, cr, ssem, rsem,
):
    me = lax.axis_index("axial")
    depth_me = lax.axis_index("dp")
    length = len_ref[0]

    barrier = pltpu.get_barrier_semaphore()

    def hello(s, _):
        pl.semaphore_signal(barrier, inc=1, device_id={"axial": partner(me, s)}, device_id_type=MESH)
        return 0

    def hello_z(s, _):
        pl.semaphore_signal(
            barrier, inc=1, device_id={"dp": (depth_me + s) % DEPTH}, device_id_type=MESH
        )
        return 0

    lax.fori_loop(0, PARTS - 1, hello, 0)
    lax.fori_loop(1, DEPTH, hello_z, 0)

    for u, (n, p, g, f) in enumerate(
        ((n1_ref, p1_ref, g1_ref, f1_ref), (n2_ref, p2_ref, g2_ref, f2_ref))
    ):
        for vec, wide in ((n, gnb), (g, ggb)):
            col = jnp.broadcast_to(vec[...], (C, C)).T
            for k in range(W // C):
                wide[u, :, k * C : (k + 1) * C] = col
        pj[u] = p[...].astype(BF16)
        pjt[u] = p[...].T.astype(BF16)
        fw[u] = f[...].astype(BF16)
        fnt[u] = f[...].T.astype(BF16)
    acc_n[...] = jnp.zeros_like(acc_n)
    acc_g[...] = jnp.zeros_like(acc_g)

    def send(src, dst, k):
        dst[me] = src[me]

        def go(s, _):
            t = partner(me, s)
            pltpu.make_async_remote_copy(
                src_ref=src.at[t], dst_ref=dst.at[me], send_sem=ssem.at[k], recv_sem=rsem.at[k],
                device_id={"axial": t}, device_id_type=MESH,
            ).start()
            return 0

        lax.fori_loop(0, PARTS - 1, go, 0)

    def arrived(src, dst, k):
        part = pl.ds(0, PARTS - 1)
        pltpu.make_async_remote_copy(
            src_ref=src.at[part], dst_ref=dst.at[part], send_sem=ssem.at[k], recv_sem=rsem.at[k],
            device_id={"axial": partner(me, 0)}, device_id_type=MESH,
        ).wait()

    def rows(body):
        lax.fori_loop(0, ROWS, lambda r, _: (body(r), 0)[1], 0)

    def alive(q, r):
        col = lax.broadcasted_iota(jnp.int32, (1, W), 1) + q * W
        row = jnp.zeros((1, W), jnp.int32) + (me * ROWS + r)
        return jnp.where(jnp.maximum(col, row) < length, 1.0, 0.0)

    def cut(q, r):
        return pl.ds(pl.multiple_of((q * ROWS + r) * W, W), W)

    def strided(r):
        return pl.ds(r, C, stride=ROWS)

    def entry(u, q, r, x):
        b = q * ROWS + r
        hat, rs = center(x)
        xh[u, b] = hat
        rsx[u, b] = rs
        normed = (hat * gnb[u]).astype(BF16)
        nrm[u, :, cut(q, r)] = normed
        mask = alive(q, r)
        for side in range(2):
            value = dot(pjt[u, side * C : (side + 1) * C, :], normed)
            sig = sigmoid(dot(pjt[u, (2 + side) * C : (3 + side) * C, :], normed))
            st[u, b, side * C : (side + 1) * C, :] = value
            st[u, b, (2 + side) * C : (3 + side) * C, :] = sig
            tmp[side, strided(r), :] = value * sig * mask
        st[u, b, 4 * C :, :] = sigmoid(dot(pjt[u, 4 * C :, :], normed))

    def leave(u, q, r):
        b = q * ROWS + r
        hat, rs = center(tmp[0, strided(r), :])
        ih[u, b] = hat
        rsi[u, b] = rs
        normed = (hat * ggb[u]).astype(BF16)
        fnn[u, :, cut(q, r)] = normed
        product = dot(fnt[u], normed)
        prod[u, b] = product
        return product

    def leave_back(u, q, r, grad):
        b = q * ROWS + r
        gate = st[u, b, 4 * C :, :]
        grad_product = (grad * gate).astype(BF16)
        gp[u, :, cut(q, r)] = grad_product
        gm[u, 4 * C :, cut(q, r)] = (grad * prod[u, b] * gate * (1.0 - gate)).astype(BF16)
        grad_normed = dot(fw[u], grad_product)
        hat = ih[u, b]
        acc_g[u] += grad_normed * hat
        tmp[0, strided(r), :] = center_back(grad_normed * ggb[u], hat, rsi[u, b])

    def entry_back(u, q, r):
        b = q * ROWS + r
        mask = alive(q, r)
        for side in range(2):
            grad = tmp[side, strided(r), :] * mask
            value = st[u, b, side * C : (side + 1) * C, :]
            sig = st[u, b, (2 + side) * C : (3 + side) * C, :]
            through = grad * sig
            gm[u, side * C : (side + 1) * C, cut(q, r)] = through.astype(BF16)
            gm[u, (2 + side) * C : (3 + side) * C, cut(q, r)] = (
                through * value * (1.0 - sig)
            ).astype(BF16)
        grad_normed = dot(pj[u], gm[u, :, cut(q, r)])
        hat = xh[u, b]
        acc_n[u] += grad_normed * hat
        return center_back(grad_normed * gnb[u], hat, rsx[u, b])

    def pack(dst, sides):
        def one(d, _):
            for side in range(sides):
                dst[d, side * 32 : (side + 1) * 32, :] = tmp[
                    side, pl.ds(pl.multiple_of(d * 32, 32), 32), :
                ].astype(BF16)
            return 0

        lax.fori_loop(0, PARTS, one, 0)

    def unpack(src, sides):
        def one(d, _):
            for side in range(sides):
                tmp[side, pl.ds(pl.multiple_of(d * 32, 32), 32), :] = src[
                    d, side * 32 : (side + 1) * 32, :
                ].astype(F32)
            return 0

        lax.fori_loop(0, PARTS, one, 0)

    def channels(ref, base, h):
        parts = [
            ref[q, :, base + 16 * h : base + 16 * h + 16, :].astype(F32).reshape(PARTS, 2, ROWS, W)
            for q in range(CHUNKS)
        ]
        return [
            jnp.concatenate([p[:, e].reshape(TOK, W) for p in parts], axis=1).astype(BF16)
            for e in range(2)
        ]

    def put(dst, base, h, both):
        both = jnp.concatenate([m.reshape(PARTS, ROWS, TOK) for m in both], axis=1).astype(BF16)
        for q in range(CHUNKS):
            dst[q, :, base + 16 * h : base + 16 * h + 16, :] = both[:, :, q * W : (q + 1) * W]

    def phase(k, q):
        return k * CHUNKS + q

    pl.semaphore_wait(barrier, PARTS - 1 + DEPTH - 1)
    for q in range(CHUNKS):

        def first(r):
            x = pair_ref[r, q * W : (q + 1) * W, :].astype(F32).T
            xt[q * ROWS + r] = x
            entry(0, q, r, x)

        rows(first)
        pack(sa.at[0, q], 2)
        send(sa.at[0, q], ra.at[0, q], phase(0, q))

    for q in range(CHUNKS):

        def turn(r):
            ct[q * ROWS + r] = cot_ref[r, q * W : (q + 1) * W, :].astype(F32).T

        rows(turn)

    def forward_triangle(u, src, dst, k):
        for q in range(CHUNKS):
            arrived(sa.at[src, q], ra.at[src, q], phase(k - 1, q))
        for h in range(2):
            left, right = channels(ra.at[src], 0, h), channels(ra.at[src], 32, h)
            for e in range(2):
                tri[u, 0, 2 * h + e] = left[e]
                tri[u, 1, 2 * h + e] = right[e]
            contract = 1 - u
            put(sb.at[dst], 0, h, [dot(left[e], right[e], contract, contract) for e in range(2)])
        for q in range(CHUNKS):
            send(sb.at[dst, q], rb.at[dst, q], phase(k, q))

    def backward_triangle(u, src, dst, k):
        for q in range(CHUNKS):
            arrived(sb.at[src, q], rb.at[src, q], phase(k - 1, q))
        for h in range(2):
            grad = channels(rb.at[src], 0, h)
            left = [tri[u, 0, 2 * h + e] for e in range(2)]
            right = [tri[u, 1, 2 * h + e] for e in range(2)]
            if u == 0:
                grad_left = [dot(grad[e], right[e]) for e in range(2)]
                grad_right = [dot(grad[e], left[e], 0, 0) for e in range(2)]
            else:
                grad_left = [dot(right[e], grad[e], 1, 1) for e in range(2)]
                grad_right = [dot(left[e], grad[e]) for e in range(2)]
            put(sa.at[dst], 0, h, grad_left)
            put(sa.at[dst], 32, h, grad_right)
        for q in range(CHUNKS):
            send(sa.at[dst, q], ra.at[dst, q], phase(k, q))

    forward_triangle(0, 0, 0, 1)

    for q in range(CHUNKS):
        arrived(sb.at[0, q], rb.at[0, q], phase(1, q))
        unpack(rb.at[0, q], 1)

        def second(r):
            b = q * ROWS + r
            product = leave(0, q, r)
            middle = (xt[b] + product * st[0, b, 4 * C :, :]).astype(BF16).astype(F32)
            entry(1, q, r, middle)

        rows(second)
        pack(sa.at[1, q], 2)
        send(sa.at[1, q], ra.at[1, q], phase(2, q))

    forward_triangle(1, 1, 1, 3)

    for q in range(CHUNKS):
        arrived(sb.at[1, q], rb.at[1, q], phase(3, q))
        unpack(rb.at[1, q], 1)

        def third(r):
            leave(1, q, r)
            leave_back(1, q, r, ct[q * ROWS + r])

        rows(third)
        pack(sb.at[2, q], 1)
        send(sb.at[2, q], rb.at[2, q], phase(4, q))

    backward_triangle(1, 2, 2, 5)

    for q in range(CHUNKS):
        arrived(sa.at[2, q], ra.at[2, q], phase(5, q))
        unpack(ra.at[2, q], 2)

        def fourth(r):
            b = q * ROWS + r
            grad = ct[b] + entry_back(1, q, r)
            ct[b] = grad
            leave_back(0, q, r, grad)

        rows(fourth)
        pack(sb.at[3, q], 1)
        send(sb.at[3, q], rb.at[3, q], phase(6, q))

    def weight_grads(u):
        proj = dot(nrm[u], gm[u], 1, 1)
        final = dot(fnn[u], gp[u], 1, 1)
        low, high = proj[:, :LANES], jnp.concatenate([proj[:, LANES:], final], axis=1)
        for i in range(C // PIECE):
            ws[i * 4 + 2 * u, :, :LANES] = low[i * PIECE : (i + 1) * PIECE].astype(BF16)
            ws[i * 4 + 2 * u + 1, :, :LANES] = high[i * PIECE : (i + 1) * PIECE].astype(BF16)

    def gain_row(acc):
        total = acc[:, :C]
        for k in range(1, W // C):
            total = total + acc[:, k * C : (k + 1) * C]
        return jnp.sum(total.T, axis=0, keepdims=True)

    weight_grads(1)

    backward_triangle(0, 3, 3, 7)

    for q in range(CHUNKS):
        arrived(sa.at[3, q], ra.at[3, q], phase(7, q))
        unpack(ra.at[3, q], 2)

        def fifth(r):
            grad = ct[q * ROWS + r] + entry_back(0, q, r)
            out_ref[r, q * W : (q + 1) * W, :] = grad.T

        rows(fifth)

    weight_grads(0)
    gains = [gain_row(acc_n[0]), gain_row(acc_g[0]), gain_row(acc_n[1]), gain_row(acc_g[1])]
    gains = jnp.concatenate(gains + [jnp.zeros((PIECE - 4, C), F32)], axis=0).astype(BF16)

    def spread(d, _):
        ws[d, :, LANES:] = gains
        return 0

    lax.fori_loop(0, PARTS, spread, 0)
    last = 8 * CHUNKS
    send(ws, wr, last)
    arrived(ws, wr, last)

    def add(ref):
        return lambda d, total: total + ref[d].astype(F32)

    zs[...] = lax.fori_loop(0, PARTS, add(wr), jnp.zeros((PIECE, LANES + C), F32)).astype(BF16)
    zr[depth_me] = zs[...]

    def go_z(s, _):
        pltpu.make_async_remote_copy(
            src_ref=zs, dst_ref=zr.at[depth_me], send_sem=ssem.at[last + 1],
            recv_sem=rsem.at[last + 1],
            device_id={"dp": (depth_me + s) % DEPTH}, device_id_type=MESH,
        ).start()
        return 0

    lax.fori_loop(1, DEPTH, go_z, 0)
    part = pl.ds(0, DEPTH - 1)
    pltpu.make_async_remote_copy(
        src_ref=zr.at[part], dst_ref=zr.at[part], send_sem=ssem.at[last + 1],
        recv_sem=rsem.at[last + 1],
        device_id={"dp": (depth_me + 1) % DEPTH}, device_id_type=MESH,
    ).wait()
    scale = 1.0 / math.sqrt(DEPTH * TOK * TOK)
    total = lax.fori_loop(0, DEPTH, add(zr), jnp.zeros((PIECE, LANES + C), F32)) * scale
    for k, ref in enumerate((on1, og1, on2, og2)):
        ref[...] = total[k : k + 1, LANES:]
    cs[...] = total[:, :LANES].astype(BF16)
    cr[me] = cs[...]

    def go_c(s, _):
        pltpu.make_async_remote_copy(
            src_ref=cs, dst_ref=cr.at[me], send_sem=ssem.at[last + 2], recv_sem=rsem.at[last + 2],
            device_id={"axial": partner(me, s)}, device_id_type=MESH,
        ).start()
        return 0

    lax.fori_loop(0, PARTS - 1, go_c, 0)
    arrived(cr, cr, last + 2)
    for u, (proj, final) in enumerate(((op1, of1), (op2, of2))):
        for i in range(C // PIECE):
            here = slice(i * PIECE, (i + 1) * PIECE)
            proj[here, :LANES] = cr[i * 4 + 2 * u].astype(F32)
            high = cr[i * 4 + 2 * u + 1].astype(F32)
            proj[here, LANES:] = high[:, : 5 * C - LANES]
            final[here, :] = high[:, 5 * C - LANES :]


def body(pair, cotangent, lengths, *weights):
    weights = [w.reshape(1, C) if w.ndim == 1 else w for w in weights]
    vmem = pl.BlockSpec(memory_space=pltpu.VMEM)
    sums = [jax.ShapeDtypeStruct(w.shape, F32) for w in weights]
    outs = pl.pallas_call(
        kernel,
        out_shape=[jax.ShapeDtypeStruct((ROWS, TOK, C), F32)] + sums,
        in_specs=[pl.BlockSpec(memory_space=pltpu.SMEM)] + [vmem] * 10,
        out_specs=[vmem] * 9,
        scratch_shapes=[
            pltpu.VMEM((2, C, W), F32),
            pltpu.VMEM((2, C, W), F32),
            pltpu.VMEM((2, 5 * C, C), BF16),
            pltpu.VMEM((2, C, 5 * C), BF16),
            pltpu.VMEM((2, C, C), BF16),
            pltpu.VMEM((2, C, C), BF16),
            pltpu.VMEM((BLOCKS, C, W), F32),
            pltpu.VMEM((BLOCKS, C, W), F32),
            pltpu.VMEM((2, BLOCKS, C, W), F32),
            pltpu.VMEM((2, BLOCKS, 1, W), F32),
            pltpu.VMEM((2, BLOCKS, 5 * C, W), F32),
            pltpu.VMEM((2, C, CELLS), BF16),
            pltpu.VMEM((2, 5 * C, CELLS), BF16),
            pltpu.VMEM((2, C, CELLS), BF16),
            pltpu.VMEM((2, C, CELLS), BF16),
            pltpu.VMEM((2, BLOCKS, C, W), F32),
            pltpu.VMEM((2, BLOCKS, 1, W), F32),
            pltpu.VMEM((2, BLOCKS, C, W), F32),
            pltpu.VMEM((2, C, W), F32),
            pltpu.VMEM((2, C, W), F32),
            pltpu.VMEM((2, C * ROWS, W), F32),
            pltpu.VMEM((4, CHUNKS, PARTS, 64, W), BF16),
            pltpu.VMEM((4, CHUNKS, PARTS, 64, W), BF16),
            pltpu.VMEM((4, CHUNKS, PARTS, 32, W), BF16),
            pltpu.VMEM((4, CHUNKS, PARTS, 32, W), BF16),
            pltpu.VMEM((2, 2, 4, TOK, TOK), BF16),
            pltpu.VMEM((PARTS, PIECE, LANES + C), BF16),
            pltpu.VMEM((PARTS, PIECE, LANES + C), BF16),
            pltpu.VMEM((PIECE, LANES + C), BF16),
            pltpu.VMEM((DEPTH, PIECE, LANES + C), BF16),
            pltpu.VMEM((PIECE, LANES), BF16),
            pltpu.VMEM((PARTS, PIECE, LANES), BF16),
            pltpu.SemaphoreType.DMA((8 * CHUNKS + 3,)),
            pltpu.SemaphoreType.DMA((8 * CHUNKS + 3,)),
        ],
        compiler_params=pltpu.CompilerParams(
            collective_id=0, has_side_effects=True, vmem_limit_bytes=60 << 20
        ),
    )(lengths, pair[0], cotangent[0], *weights)
    grads = [o.reshape(C) if o.shape[0] == 1 else o for o in outs[1:]]
    return (outs[0][None], *grads)


def solution(mesh):
    return jax.shard_map(
        body,
        mesh=mesh,
        in_specs=(P("dp", "axial", None, None), P("dp", "axial", None, None), P("dp")) + (P(),) * 8,
        out_specs=(P("dp", "axial", None, None),) + (P(),) * 8,
        check_vma=False,
    )
```

time: 855 us -> 172 us (0.20)
  waiting for transfers between devices: 515 us -> 0 us
  blocking collectives: 181 us -> 0 us
  Pallas kernels: 0 us -> 163 us
  other arithmetic: 39.2 us -> 0 us
  starting transfers between devices: 35.2 us -> 0 us
  matrix products: 30.6 us -> 0 us
  local copies, waits for them, and re-layouts: 36.3 us -> 7.14 us
  between operations: 15.4 us -> 1.33 us
    psum x1 -> x0, waiting for transfers between devices: 459 us -> none  [body(): lax.psum((grad_norm_one, grad_proj_one, grad_gain_one, grad_final_one), (...]
    pallas_call x0 -> x1, Pallas kernels: none -> 163 us  [body(): pl.pallas_call(kernel, out_shape=[jax.ShapeDtypeStruct((ROWS, TOK, C), F3...]
    psum x1 -> x0, blocking collectives: 105 us -> none  [body(): lax.psum((grad_norm_one, grad_proj_one, grad_gain_one, grad_final_one), (...]
    all_to_all x5 -> x0, blocking collectives: 75.7 us -> none  [the longest x1 15.2 us: body(): lax.all_to_all(left_second, 'axial', split_axis=0, concat_axis=1, tiled=T...]
    all_to_all x7 -> x0, waiting for transfers between devices: 55.6 us -> none  [the longest x1 11.3 us: body(): lax.all_to_all(right_first, 'axial', split_axis=0, concat_axis=1, tiled=T...]
    all_to_all x7 -> x0, starting transfers between devices: 34.9 us -> none  [the longest x1 10.4 us: body(): lax.all_to_all(right_first, 'axial', split_axis=0, concat_axis=1, tiled=T...]
    dot_general x18 -> x0, matrix products: 30.6 us -> none  [the longest x2 5.6 us: leave(): jnp.dot(final_normed, final_weight.astype(jnp.bfloat16), preferred_elemen...]
    reshape x14 -> x0, local copies, waits for them, and re-layouts: 20.4 us -> none  [the longest x8 12.9 us: row_major(): return jnp.transpose(field, (1, 2, 0)).reshape(-1, hidden)]
  transfers between devices with their start and end apart: 8 -> 0, of which waited for: 8 -> 0; matrix products, arithmetic and copies ran while one was open for 3% -> 0% of each run, Pallas kernels for 0% -> 0%
where the time goes in v1:
time: 172 us
  Pallas kernels  163 us (95%)
  local copies, waits for them, and re-layouts  7.14 us (4%)
    pallas_call x1, Pallas kernels, body(): pl.pallas_call(kernel, out_shape=[jax.ShapeDtypeStruct((ROWS, TOK, C), F3...  163 us
    unnamed x25, local copies, waits for them, and re-layouts  7.14 us

profile of v1, /device:TPU:1, one launch (start us, length us, event | category | flops | bytes accessed | tf_op | source)
XLA Modules:
  0.0 171.7 jit_solution(6056674030049915734)
XLA Ops:
  1.3 163.3 %shard_map.178 = (f32[8,256,128]{2,1,0:T(8,128)}, f32[1,128]{1,0:T(1,128)}, f32[128,640]{1,0:T(8,128)}, f32[1,128]{1,0:T(1,128)}, f32[128,128]{1,0:T(8,128)}, /*...) custom-call(s32[1]{0:T(128)S(6)} %copy.29.len_ref, ...), custom_call_target="tpu_custom_call" | custom-call | tf_op jit(solution)/shard_map/pallas_call | solution.py:406
  164.6 0.0 copy-start.7
  164.6 0.0 copy-start.1
  164.6 2.3 %copy.30 = f32[1,8,256,128]{3,2,1,0:T(8,128)} copy(f32[1,8,256,128]{3,2,1,0:T(8,128)} %bitcast.11) | data formatting | bytes 2097152
  166.9 0.0 copy-done.7
  166.9 0.5 copy.31
  167.4 0.0 copy-done.1
  167.4 0.0 copy-start.6
  167.4 0.0 copy-start.3
  167.4 0.0 copy-start
  167.4 0.7 copy.32
  168.2 0.0 copy-done.6
  168.2 0.5 copy.33
  168.7 0.0 copy-done.3
  168.7 0.0 copy-start.5
  168.7 0.6 copy.34
  169.3 0.0 copy-done.5
  169.3 0.5 copy.35
  169.9 0.0 copy-done
  169.9 0.0 copy-start.4
  169.9 0.0 copy-start.2
  169.9 0.7 copy.36
  170.6 0.0 copy-done.4
  170.6 0.5 copy.37
  171.1 0.0 copy-done.2
  171.1 0.6 copy.38
Async XLA Ops:
  164.6 2.3 %copy-start.7 = (f32[1,128]{1,0:T(1,128)S(1)}, f32[1,128]{1,0:T(1,128)}, u32[]{:S(2)}) copy-start(f32[1,128]{1,0:T(1,128)} %get-tuple-element.19) | copy-start | bytes 1540
  164.6 2.8 %copy-start.1 = (f32[128,640]{1,0:T(8,128)S(1)}, f32[128,640]{1,0:T(8,128)}, u32[]{:S(2)}) copy-start(f32[128,640]{1,0:T(8,128)} %get-tuple-element.38) | copy-start | bytes 983044
  167.4 0.7 copy-start.6
  167.4 1.3 copy-start.3
  167.4 2.4 %copy-start = (f32[128,640]{1,0:T(8,128)S(1)}, f32[128,640]{1,0:T(8,128)}, u32[]{:S(2)}) copy-start(f32[128,640]{1,0:T(8,128)} %get-tuple-element.42) | copy-start | bytes 983044
  168.7 0.7 copy-start.5
  169.9 0.7 copy-start.4
  169.9 1.2 copy-start.2

commit v2 on v1

v2 whole, which is shorter than its diff:
```python
import functools
import math

import jax
import jax.numpy as jnp
from jax import lax
from jax.experimental import pallas as pl
from jax.experimental.pallas import tpu as pltpu
from jax.sharding import PartitionSpec as P

EPSILON = 1e-05
MESH = pl.DeviceIdType.MESH
F32, BF16 = jnp.float32, jnp.bfloat16
PARTS = 32
DEPTH = 16
ROWS, TOK, C = 8, 256, 128
CHUNKS = 2
W = TOK // CHUNKS
BLOCKS = ROWS * CHUNKS
CELLS = ROWS * TOK
PIECE = 16
EARLY, LATE = 256, 128


def dot(a, b, ca=1, cb=0):
    return lax.dot_general(a, b, (((ca,), (cb,)), ((), ())), preferred_element_type=F32)


def sigmoid(v):
    return 0.5 * jnp.tanh(0.5 * v) + 0.5


def center(v):
    c = v - jnp.mean(v, axis=0, keepdims=True)
    rs = lax.rsqrt(jnp.mean(c * c, axis=0, keepdims=True) + EPSILON)
    return c * rs, rs


def center_back(grad, hat, rs):
    return rs * (
        grad
        - jnp.mean(grad, axis=0, keepdims=True)
        - hat * jnp.mean(grad * hat, axis=0, keepdims=True)
    )


def partner(me, s):
    u = s + lax.div(s, 20)
    ox, oy, oc = lax.div(u, 8), lax.rem(lax.div(u, 2), 4), lax.rem(u, 2)
    x, y, c = lax.div(me, 8), lax.rem(lax.div(me, 2), 4), lax.rem(me, 2)
    x, y, c = lax.rem(x + 2 + 3 * ox, 4), lax.rem(y + 2 + 3 * oy, 4), lax.rem(c + oc, 2)
    return x * 8 + y * 2 + c


def kernel(
    len_ref, pair_hbm, cot_hbm, n1_hbm, p1_hbm, g1_hbm, f1_hbm, n2_hbm, p2_hbm, g2_hbm, f2_hbm,
    out_hbm, early_out, late_out,
    pair_ref, cot_ref, n_in, p_in, g_in, f_in, out_ref,
    gnb, ggb, pjt, pj, fnt, fw, xt, ct, xh, rsx, st, nrm, gm, fnn, gp, ih, rsi, prod,
    tmp, s2, r2, s1, r1, t1, u1, t2, u2, tri, es, er, ezs, ezr, ecs, ecr, ls, lr, lzs, lzr, lcs, lcr,
    ssem, rsem, isem, osem,
):
    me = lax.axis_index("axial")
    depth_me = lax.axis_index("dp")
    length = len_ref[0]

    barrier = pltpu.get_barrier_semaphore()

    def hello(s, _):
        pl.semaphore_signal(barrier, inc=1, device_id={"axial": partner(me, s)}, device_id_type=MESH)
        return 0

    def hello_z(s, _):
        pl.semaphore_signal(
            barrier, inc=1, device_id={"dp": (depth_me + s) % DEPTH}, device_id_type=MESH
        )
        return 0

    lax.fori_loop(0, PARTS - 1, hello, 0)
    lax.fori_loop(1, DEPTH, hello_z, 0)

    loads = [(pair_hbm, pair_ref), (cot_hbm, cot_ref)]
    for u, group in enumerate(
        ((n1_hbm, p1_hbm, g1_hbm, f1_hbm), (n2_hbm, p2_hbm, g2_hbm, f2_hbm))
    ):
        loads += [(h, v.at[u]) for h, v in zip(group, (n_in, p_in, g_in, f_in))]
    loads = [pltpu.make_async_copy(h, v, isem.at[i]) for i, (h, v) in enumerate(loads)]
    for i in (2, 3, 0, 4, 5, 6, 7, 8, 9, 1):
        loads[i].start()

    def weights(u):
        for k in range(4):
            loads[2 + 4 * u + k].wait()
        for vec, wide in ((n_in, gnb), (g_in, ggb)):
            wide[u] = jnp.broadcast_to(vec[u], (C, C)).T
        pj[u] = p_in[u].astype(BF16)
        pjt[u] = p_in[u].T.astype(BF16)
        fw[u] = f_in[u].astype(BF16)
        fnt[u] = f_in[u].T.astype(BF16)

    weights(0)
    loads[0].wait()

    def send(src, dst, k):
        dst[me] = src[me]

        def go(s, _):
            t = partner(me, s)
            pltpu.make_async_remote_copy(
                src_ref=src.at[t], dst_ref=dst.at[me], send_sem=ssem.at[k], recv_sem=rsem.at[k],
                device_id={"axial": t}, device_id_type=MESH,
            ).start()
            return 0

        lax.fori_loop(0, PARTS - 1, go, 0)

    def arrived(src, dst, k):
        part = pl.ds(0, PARTS - 1)
        pltpu.make_async_remote_copy(
            src_ref=src.at[part], dst_ref=dst.at[part], send_sem=ssem.at[k], recv_sem=rsem.at[k],
            device_id={"axial": partner(me, 0)}, device_id_type=MESH,
        ).wait()

    def rows(body):
        lax.fori_loop(0, ROWS, lambda r, _: (body(r), 0)[1], 0, unroll=4)

    def alive(q, r):
        col = lax.broadcasted_iota(jnp.int32, (1, W), 1) + q * W
        row = jnp.zeros((1, W), jnp.int32) + (me * ROWS + r)
        return jnp.where(jnp.maximum(col, row) < length, 1.0, 0.0)

    def cut(q, r):
        return pl.ds(pl.multiple_of((q * ROWS + r) * W, W), W)

    def strided(r):
        return pl.ds(r, C, stride=ROWS)

    def entry(u, q, r, x):
        b = q * ROWS + r
        hat, rs = center(x)
        xh[u, b] = hat
        rsx[u, b] = rs
        normed = (hat * gnb[u]).astype(BF16)
        nrm[u, :, cut(q, r)] = normed
        mask = alive(q, r)
        for side in range(2):
            value = dot(pjt[u, side * C : (side + 1) * C, :], normed)
            sig = sigmoid(dot(pjt[u, (2 + side) * C : (3 + side) * C, :], normed))
            st[u, b, side * C : (side + 1) * C, :] = value
            st[u, b, (2 + side) * C : (3 + side) * C, :] = sig
            tmp[side, strided(r), :] = value * sig * mask
        st[u, b, 4 * C :, :] = sigmoid(dot(pjt[u, 4 * C :, :], normed))

    def leave(u, q, r):
        b = q * ROWS + r
        hat, rs = center(tmp[0, strided(r), :])
        ih[u, b] = hat
        rsi[u, b] = rs
        normed = (hat * ggb[u]).astype(BF16)
        fnn[u, :, cut(q, r)] = normed
        product = dot(fnt[u], normed)
        prod[u, b] = product
        return product

    def leave_back(u, q, r, grad):
        b = q * ROWS + r
        gate = st[u, b, 4 * C :, :]
        grad_product = (grad * gate).astype(BF16)
        gp[u, :, cut(q, r)] = grad_product
        gm[u, 4 * C :, cut(q, r)] = (grad * prod[u, b] * gate * (1.0 - gate)).astype(BF16)
        grad_normed = dot(fw[u], grad_product)
        hat = ih[u, b]
        tmp[0, strided(r), :] = center_back(grad_normed * ggb[u], hat, rsi[u, b])

    def gating_back(u, q, r):
        b = q * ROWS + r
        mask = alive(q, r)
        for side in range(2):
            grad = tmp[side, strided(r), :] * mask
            value = st[u, b, side * C : (side + 1) * C, :]
            sig = st[u, b, (2 + side) * C : (3 + side) * C, :]
            through = grad * sig
            gm[u, side * C : (side + 1) * C, cut(q, r)] = through.astype(BF16)
            gm[u, (2 + side) * C : (3 + side) * C, cut(q, r)] = (
                through * value * (1.0 - sig)
            ).astype(BF16)

    def entry_back(u, q, r):
        b = q * ROWS + r
        grad_normed = dot(pj[u], gm[u, :, cut(q, r)])
        hat = xh[u, b]
        return center_back(grad_normed * gnb[u], hat, rsx[u, b])

    def pack(dst, q, sides):
        def one(d, _):
            for p in range(2):
                for side in range(sides):
                    dst[q, d, p, side * 16 : (side + 1) * 16, :] = tmp[
                        side, pl.ds(pl.multiple_of(d * 32 + p * 16, 16), 16), :
                    ].astype(BF16)
            return 0

        lax.fori_loop(0, PARTS, one, 0, unroll=4)

    def unpack(src, q, sides):
        def one(d, _):
            for p in range(2):
                for side in range(sides):
                    tmp[side, pl.ds(pl.multiple_of(d * 32 + p * 16, 16), 16), :] = src[
                        p, d, q, side * 16 : (side + 1) * 16, :
                    ].astype(F32)
            return 0

        lax.fori_loop(0, PARTS, one, 0, unroll=4)

    def send_part(src, dst, k, part):
        if part == 0:
            send(src.at[0], dst.at[0], 3 * k)
        else:
            send(src.at[1, :, part - 1], dst.at[1, :, part - 1], 3 * k + part)

    def arrived_part(src, dst, k, part):
        if part == 0:
            arrived(src.at[0], dst.at[0], 3 * k)
        else:
            arrived(src.at[1, :, part - 1], dst.at[1, :, part - 1], 3 * k + part)

    def send_chunk(src, dst, k, chunk):
        for part in ((0,), (1, 2))[chunk]:
            send_part(src, dst, k, part)

    def arrived_half(src, dst, k, half):
        for part in ((0, 1), (2,))[half]:
            arrived_part(src, dst, k, part)

    def channels(ref, side, p, q, to):
        block = ref[q, :, p, 16 * side : 16 * side + 16, :].astype(F32)
        block = block.reshape(PARTS, 2, ROWS, W)
        for e in range(2):
            to[2 * p + e, :, q * W : (q + 1) * W] = block[:, e].reshape(TOK, W).astype(BF16)

    def put(dst, side, p, both):
        both = jnp.concatenate([m.reshape(PARTS, ROWS, TOK) for m in both], axis=1).astype(BF16)
        for q in range(CHUNKS):
            dst[p, :, q, 16 * side : 16 * side + 16, :] = both[:, :, q * W : (q + 1) * W]

    for q in range(CHUNKS):

        def first(r):
            x = pair_ref[r, q * W : (q + 1) * W, :].astype(F32).T
            xt[q * ROWS + r] = x
            entry(0, q, r, x)

        rows(first)
        pack(s2.at[0], q, 2)
        if q == 0:
            pl.semaphore_wait(barrier, PARTS - 1 + DEPTH - 1)
        send_chunk(s2.at[0], r2.at[0], 0, q)

    weights(1)
    loads[1].wait()

    for q in range(CHUNKS):

        def turn(r):
            ct[q * ROWS + r] = cot_ref[r, q * W : (q + 1) * W, :].astype(F32).T

        rows(turn)

    def forward_triangle(u, k):
        src, dst = (s2.at[u], r2.at[u]), (t1.at[u], u1.at[u])
        arrived_part(*src, k - 1, 0)
        for p in range(2):
            for side in range(2):
                channels(src[1], side, p, 0, tri.at[u, side])
        for p in range(2):
            arrived_part(*src, k - 1, 1 + p)
            for side in range(2):
                channels(src[1], side, p, 1, tri.at[u, side])
            both = [
                dot(tri[u, 0, 2 * p + e], tri[u, 1, 2 * p + e], 1 - u, 1 - u) for e in range(2)
            ]
            put(dst[0], 0, p, both)
            send_chunk(*dst, k, p)

    def backward_triangle(u, k):
        src, dst = (s1.at[u], r1.at[u]), (t2.at[u], u2.at[u])
        arrived_part(*src, k - 1, 0)
        for p in range(2):
            channels(src[1], 0, p, 0, tri.at[2, 0])
        for p in range(2):
            arrived_part(*src, k - 1, 1 + p)
            channels(src[1], 0, p, 1, tri.at[2, 0])
            grad = [tri[2, 0, 2 * p + e] for e in range(2)]
            left = [tri[u, 0, 2 * p + e] for e in range(2)]
            right = [tri[u, 1, 2 * p + e] for e in range(2)]
            if u == 0:
                grad_left = [dot(grad[e], right[e]) for e in range(2)]
                grad_right = [dot(grad[e], left[e], 0, 0) for e in range(2)]
            else:
                grad_left = [dot(right[e], grad[e], 1, 1) for e in range(2)]
                grad_right = [dot(left[e], grad[e]) for e in range(2)]
            put(dst[0], 0, p, grad_left)
            put(dst[0], 1, p, grad_right)
            send_chunk(*dst, k, p)

    forward_triangle(0, 1)

    for q in range(CHUNKS):
        arrived_half(t1.at[0], u1.at[0], 1, q)
        unpack(u1.at[0], q, 1)

        def second(r):
            b = q * ROWS + r
            product = leave(0, q, r)
            middle = (xt[b] + product * st[0, b, 4 * C :, :]).astype(BF16).astype(F32)
            entry(1, q, r, middle)

        rows(second)
        pack(s2.at[1], q, 2)
        send_chunk(s2.at[1], r2.at[1], 2, q)

    forward_triangle(1, 3)

    for q in range(CHUNKS):
        arrived_half(t1.at[1], u1.at[1], 3, q)
        unpack(u1.at[1], q, 1)

        def third(r):
            leave(1, q, r)
            leave_back(1, q, r, ct[q * ROWS + r])

        rows(third)
        pack(s1.at[1], q, 1)
        send_chunk(s1.at[1], r1.at[1], 4, q)

    backward_triangle(1, 5)

    for q in range(CHUNKS):
        arrived_half(t2.at[1], u2.at[1], 5, q)
        unpack(u2.at[1], q, 2)

        def fourth(r):
            b = q * ROWS + r
            gating_back(1, q, r)
            grad = ct[b] + entry_back(1, q, r)
            ct[b] = grad
            leave_back(0, q, r, grad)

        rows(fourth)
        pack(s1.at[0], q, 1)
        send_chunk(s1.at[0], r1.at[0], 6, q)

    last = 8 * 3

    def pieces(to, grads):
        wide = grads.shape[1] // 4
        for d in range(PARTS):
            here = grads[d // 4 * PIECE : (d // 4 + 1) * PIECE, d % 4 * wide : (d % 4 + 1) * wide]
            to[d] = here.astype(BF16)

    def total(ref):
        rest = range(1, ref.shape[0])
        return functools.reduce(lambda a, d: a + ref[d].astype(F32), rest, ref[0].astype(F32))

    def send_z(src, dst, k):
        dst[depth_me] = src[...]

        def go(s, _):
            pltpu.make_async_remote_copy(
                src_ref=src, dst_ref=dst.at[depth_me], send_sem=ssem.at[k], recv_sem=rsem.at[k],
                device_id={"dp": lax.rem(depth_me + s, DEPTH)}, device_id_type=MESH,
            ).start()
            return 0

        lax.fori_loop(1, DEPTH, go, 0)

    def arrived_z(dst, k):
        part = pl.ds(0, DEPTH - 1)
        pltpu.make_async_remote_copy(
            src_ref=dst.at[part], dst_ref=dst.at[part], send_sem=ssem.at[k], recv_sem=rsem.at[k],
            device_id={"dp": lax.rem(depth_me + 1, DEPTH)}, device_id_type=MESH,
        ).wait()

    def send_all(src, dst, k):
        dst[me] = src[...]

        def go(s, _):
            pltpu.make_async_remote_copy(
                src_ref=src, dst_ref=dst.at[me], send_sem=ssem.at[k], recv_sem=rsem.at[k],
                device_id={"axial": partner(me, s)}, device_id_type=MESH,
            ).start()
            return 0

        lax.fori_loop(0, PARTS - 1, go, 0)

    early = [
        dot(nrm[1], gm[1], 1, 1),
        dot(fnn[1], gp[1], 1, 1),
        dot(nrm[0], gm[0, 4 * C :, :], 1, 1),
        dot(fnn[0], gp[0], 1, 1),
    ]
    pieces(es, jnp.concatenate(early, axis=1))
    send(es, er, last)

    backward_triangle(0, 7)

    arrived(es, er, last)
    ezs[...] = total(er).astype(BF16)
    send_z(ezs, ezr, last + 1)

    def store(q):
        here = (slice(None), pl.ds(q * W, W))
        return pltpu.make_async_copy(out_ref.at[here], out_hbm.at[here], osem.at[q])

    def fifth(q, r):
        grad = ct[q * ROWS + r] + entry_back(0, q, r)
        out_ref[r, q * W : (q + 1) * W, :] = grad.T

    for q in range(CHUNKS):
        arrived_half(t2.at[0], u2.at[0], 7, q)
        unpack(u2.at[0], q, 2)
        rows(functools.partial(gating_back, 0, q))
        if q == 0:
            rows(functools.partial(fifth, q))
            store(q).start()

    scale = 1.0 / math.sqrt(DEPTH * TOK * TOK)
    pieces(ls, dot(nrm[0], gm[0, : 4 * C, :], 1, 1))
    send(ls, lr, last + 3)
    rows(functools.partial(fifth, 1))
    store(1).start()
    arrived_z(ezr, last + 1)
    ecs[...] = (total(ezr) * scale).astype(BF16)
    arrived(ls, lr, last + 3)
    lzs[...] = total(lr).astype(BF16)
    send_z(lzs, lzr, last + 4)
    send_all(ecs, ecr, last + 2)
    arrived_z(lzr, last + 4)
    lcs[...] = (total(lzr) * scale).astype(BF16)
    send_all(lcs, lcr, last + 5)
    arrived(ecr, ecr, last + 2)
    early_out[...] = ecr[...]
    for q in range(CHUNKS):
        store(q).wait()
    arrived(lcr, lcr, last + 5)
    late_out[...] = lcr[...]


def finish(
    big, early, late, n1, p1, g1, f1, n2, p2, g2, f2, out, on1, op1, og1, of1, on2, op2, og2, of2
):
    out[...] = big[...]
    for i in range(C // PIECE):
        here = slice(i * PIECE, (i + 1) * PIECE)
        blocks = [early[4 * i + j].astype(F32) for j in range(4)]
        for j in range(4):
            op1[here, j * LATE : (j + 1) * LATE] = late[4 * i + j].astype(F32)
        op1[here, 4 * C :] = blocks[3][:, :C]
        of1[here, :] = blocks[3][:, C:]
        op2[here, : 2 * C] = blocks[0]
        op2[here, 2 * C : 4 * C] = blocks[1]
        op2[here, 4 * C :] = blocks[2][:, :C]
        of2[here, :] = blocks[2][:, C:]

    def gain(to, by, weight, grad):
        both = weight[...].astype(BF16).astype(F32) * grad[...]
        both = sum(both[:, j * C : (j + 1) * C] for j in range(both.shape[1] // C))
        to[...] = jnp.sum(both.T, axis=0, keepdims=True) / by[...]

    gain(on1, n1, p1, op1)
    gain(og1, g1, f1, of1)
    gain(on2, n2, p2, op2)
    gain(og2, g2, f2, of2)


def body(pair, cotangent, lengths, *weights):
    weights = [w.reshape(1, C) if w.ndim == 1 else w for w in weights]
    vmem = pl.BlockSpec(memory_space=pltpu.VMEM)
    sums = [jax.ShapeDtypeStruct(w.shape, F32) for w in weights]
    hbm = pl.BlockSpec(memory_space=pl.ANY)
    parts = pl.pallas_call(
        kernel,
        out_shape=[
            jax.ShapeDtypeStruct((ROWS, TOK, C), F32),
            jax.ShapeDtypeStruct((PARTS, PIECE, EARLY), BF16),
            jax.ShapeDtypeStruct((PARTS, PIECE, LATE), BF16),
        ],
        in_specs=[pl.BlockSpec(memory_space=pltpu.SMEM)] + [hbm] * 10,
        out_specs=[hbm, vmem, vmem],
        scratch_shapes=[
            pltpu.VMEM((ROWS, TOK, C), BF16),
            pltpu.VMEM((ROWS, TOK, C), BF16),
            pltpu.VMEM((2, 1, C), F32),
            pltpu.VMEM((2, C, 5 * C), F32),
            pltpu.VMEM((2, 1, C), F32),
            pltpu.VMEM((2, C, C), F32),
            pltpu.VMEM((ROWS, TOK, C), F32),
            pltpu.VMEM((2, C, W), F32),
            pltpu.VMEM((2, C, W), F32),
            pltpu.VMEM((2, 5 * C, C), BF16),
            pltpu.VMEM((2, C, 5 * C), BF16),
            pltpu.VMEM((2, C, C), BF16),
            pltpu.VMEM((2, C, C), BF16),
            pltpu.VMEM((BLOCKS, C, W), F32),
            pltpu.VMEM((BLOCKS, C, W), F32),
            pltpu.VMEM((2, BLOCKS, C, W), F32),
            pltpu.VMEM((2, BLOCKS, 1, W), F32),
            pltpu.VMEM((2, BLOCKS, 5 * C, W), F32),
            pltpu.VMEM((2, C, CELLS), BF16),
            pltpu.VMEM((2, 5 * C, CELLS), BF16),
            pltpu.VMEM((2, C, CELLS), BF16),
            pltpu.VMEM((2, C, CELLS), BF16),
            pltpu.VMEM((2, BLOCKS, C, W), F32),
            pltpu.VMEM((2, BLOCKS, 1, W), F32),
            pltpu.VMEM((2, BLOCKS, C, W), F32),
            pltpu.VMEM((2, C * ROWS, W), F32),
        ]
        + [
            pltpu.VMEM((2, 2, PARTS, 2, 16 * sides, W), BF16)
            for sides in (2, 2, 1, 1, 1, 1, 2, 2)
        ]
        + [
            pltpu.VMEM((3, 2, 4, TOK, TOK), BF16),
        ]
        + [
            pltpu.VMEM(shape + (PIECE, wide), BF16)
            for wide in (EARLY, LATE)
            for shape in ((PARTS,), (PARTS,), (), (DEPTH,), (), (PARTS,))
        ]
        + [
            pltpu.SemaphoreType.DMA((8 * 3 + 6,)),
            pltpu.SemaphoreType.DMA((8 * 3 + 6,)),
            pltpu.SemaphoreType.DMA((10,)),
            pltpu.SemaphoreType.DMA((CHUNKS,)),
        ],
        compiler_params=pltpu.CompilerParams(
            collective_id=0, has_side_effects=True, vmem_limit_bytes=60 << 20
        ),
    )(lengths, pair[0], cotangent[0], *weights)
    outs = pl.pallas_call(
        finish,
        out_shape=[jax.ShapeDtypeStruct((ROWS, TOK, C), F32)] + sums,
        in_specs=[vmem] * 11,
        out_specs=[vmem] * 9,
        compiler_params=pltpu.CompilerParams(vmem_limit_bytes=60 << 20),
    )(*parts, *weights)
    grads = [o.reshape(C) if o.shape[0] == 1 else o for o in outs[1:]]
    return (outs[0][None], *grads)


def solution(mesh):
    return jax.shard_map(
        body,
        mesh=mesh,
        in_specs=(P("dp", "axial", None, None), P("dp", "axial", None, None), P("dp")) + (P(),) * 8,
        out_specs=(P("dp", "axial", None, None),) + (P(),) * 8,
        check_vma=False,
    )
```

time: 172 us -> 136 us (0.79)
  Pallas kernels: 163 us -> 134 us
  local copies, waits for them, and re-layouts: 7.14 us -> 0 us
    pallas_call x1, Pallas kernels: 163 us -> 131 us  [body(): pl.pallas_call(kernel, out_shape=[jax.ShapeDtypeStruct((ROWS, TOK, C), F3...]
    unnamed x25 -> x0, local copies, waits for them, and re-layouts: 7.14 us -> none
    pallas_call x0 -> x1, Pallas kernels: none -> 2.97 us  [body(): pl.pallas_call(finish, out_shape=[jax.ShapeDtypeStruct((ROWS, TOK, C), F3...]
where the time goes in v2:
time: 136 us
  Pallas kernels  134 us (99%)
    pallas_call x1, Pallas kernels, body(): pl.pallas_call(kernel, out_shape=[jax.ShapeDtypeStruct((ROWS, TOK, C), F3...  131 us
    pallas_call x1, Pallas kernels, body(): pl.pallas_call(finish, out_shape=[jax.ShapeDtypeStruct((ROWS, TOK, C), F3...  2.97 us

profile of v2, /device:TPU:1, one launch (start us, length us, event | category | flops | bytes accessed | tf_op | source)
XLA Modules:
  0.0 135.7 jit_solution(7096811511922817771)
XLA Ops:
  1.3 131.4 %shard_map.178 = (f32[8,256,128]{2,1,0:T(8,128)}, bf16[32,16,256]{2,1,0:T(8,128)(2,1)}, bf16[32,16,128]{2,1,0:T(8,128)(2,1)}) custom-call(s32[1]{0:T(128)S(6)} %copy.20.len_ref, bf16[8,256,128]{2,1,0:T(8,128)(2,1)} %bitcast.11, bf16[8,256,128]{2,1,0:T(8,128)(2,1)} %bitcast.12, f32[1,128]{1,0:T(1,128)} %bitcast.13, f32[128,640]{1,0:T(8,128)} %p1.1, ...), custom_call_target="tpu_custom_call" | custom-call | tf_op jit(solution)/shard_map/pallas_call | solution.py:482
  132.7 3.0 %shard_map.179 = (f32[8,256,128]{2,1,0:T(8,128)}, f32[1,128]{1,0:T(1,128)}, f32[128,640]{1,0:T(8,128)}, f32[1,128]{1,0:T(1,128)}, f32[128,128]{1,0:T(8,128)}, /*...) custom-call(f32[8,256,128]{2,1,0:T(8,128)} %get-tuple-element.21.big, ...), custom_call_target="tpu_custom_call" | custom-call | tf_op jit(solution)/shard_map/pallas_call | solution.py:541

commit v3 on v2

--- a/solution.py
+++ b/solution.py
@@ -44,12 +44,23 @@
     )
 
 
-def partner(me, s):
-    u = s + lax.div(s, 20)
-    ox, oy, oc = lax.div(u, 8), lax.rem(lax.div(u, 2), 4), lax.rem(u, 2)
+FAR = (10, 6, 9, 11, 14, 2, 5, 7, 8, 13, 15, 1, 3, 4, 12)
+
+
+def each_partner(me, act):
     x, y, c = lax.div(me, 8), lax.rem(lax.div(me, 2), 4), lax.rem(me, 2)
-    x, y, c = lax.rem(x + 2 + 3 * ox, 4), lax.rem(y + 2 + 3 * oy, 4), lax.rem(c + oc, 2)
-    return x * 8 + y * 2 + c
+
+    def chip(_, codes):
+        code = lax.rem(codes, 16)
+        there = lax.rem(x + lax.div(code, 4), 4) * 8 + lax.rem(y + lax.rem(code, 4), 4) * 2
+        act(there)
+        act(there + 1)
+        return lax.div(codes, 16)
+
+    for part in (FAR[:5], FAR[5:10], FAR[10:]):
+        codes = sum(code * 16**k for k, code in enumerate(part))
+        lax.fori_loop(0, len(part), chip, jnp.int32(codes))
+    act(me + 1 - 2 * c)
 
 
 def kernel(
@@ -58,7 +69,7 @@
     pair_ref, cot_ref, n_in, p_in, g_in, f_in, out_ref,
     gnb, ggb, pjt, pj, fnt, fw, xt, ct, xh, rsx, st, nrm, gm, fnn, gp, ih, rsi, prod,
     tmp, s2, r2, s1, r1, t1, u1, t2, u2, tri, es, er, ezs, ezr, ecs, ecr, ls, lr, lzs, lzr, lcs, lcr,
-    ssem, rsem, isem, osem,
+    share, ssem, rsem, isem, osem,
 ):
     me = lax.axis_index("axial")
     depth_me = lax.axis_index("dp")
@@ -66,9 +77,8 @@
 
     barrier = pltpu.get_barrier_semaphore()
 
-    def hello(s, _):
-        pl.semaphore_signal(barrier, inc=1, device_id={"axial": partner(me, s)}, device_id_type=MESH)
-        return 0
+    def hello(t):
+        pl.semaphore_signal(barrier, inc=1, device_id={"axial": t}, device_id_type=MESH)
 
     def hello_z(s, _):
         pl.semaphore_signal(
@@ -76,8 +86,8 @@
         )
         return 0
 
-    lax.fori_loop(0, PARTS - 1, hello, 0)
     lax.fori_loop(1, DEPTH, hello_z, 0)
+    each_partner(me, hello)
 
     loads = [(pair_hbm, pair_ref), (cot_hbm, cot_ref)]
     for u, group in enumerate(
@@ -104,21 +114,19 @@
     def send(src, dst, k):
         dst[me] = src[me]
 
-        def go(s, _):
-            t = partner(me, s)
+        def go(t):
             pltpu.make_async_remote_copy(
                 src_ref=src.at[t], dst_ref=dst.at[me], send_sem=ssem.at[k], recv_sem=rsem.at[k],
                 device_id={"axial": t}, device_id_type=MESH,
             ).start()
-            return 0
-
-        lax.fori_loop(0, PARTS - 1, go, 0)
+
+        each_partner(me, go)
 
     def arrived(src, dst, k):
         part = pl.ds(0, PARTS - 1)
         pltpu.make_async_remote_copy(
             src_ref=src.at[part], dst_ref=dst.at[part], send_sem=ssem.at[k], recv_sem=rsem.at[k],
-            device_id={"axial": partner(me, 0)}, device_id_type=MESH,
+            device_id={"axial": lax.rem(me + 1, PARTS)}, device_id_type=MESH,
         ).wait()
 
     def rows(body):
@@ -195,7 +203,7 @@
         def one(d, _):
             for p in range(2):
                 for side in range(sides):
-                    dst[q, d, p, side * 16 : (side + 1) * 16, :] = tmp[
+                    dst[p, d, q, side * 16 : (side + 1) * 16, :] = tmp[
                         side, pl.ds(pl.multiple_of(d * 32 + p * 16, 16), 16), :
                     ].astype(BF16)
             return 0
@@ -207,34 +215,28 @@
             for p in range(2):
                 for side in range(sides):
                     tmp[side, pl.ds(pl.multiple_of(d * 32 + p * 16, 16), 16), :] = src[
-                        p, d, q, side * 16 : (side + 1) * 16, :
+                        q, d, p, side * 16 : (side + 1) * 16, :
                     ].astype(F32)
             return 0
 
         lax.fori_loop(0, PARTS, one, 0, unroll=4)
 
-    def send_part(src, dst, k, part):
-        if part == 0:
-            send(src.at[0], dst.at[0], 3 * k)
-        else:
-            send(src.at[1, :, part - 1], dst.at[1, :, part - 1], 3 * k + part)
-
-    def arrived_part(src, dst, k, part):
-        if part == 0:
-            arrived(src.at[0], dst.at[0], 3 * k)
-        else:
-            arrived(src.at[1, :, part - 1], dst.at[1, :, part - 1], 3 * k + part)
+    def part(ref, i):
+        return ref.at[1] if i == 2 else ref.at[0, :, i]
 
     def send_chunk(src, dst, k, chunk):
-        for part in ((0,), (1, 2))[chunk]:
-            send_part(src, dst, k, part)
+        for i in ((0,), (1, 2))[chunk]:
+            send(part(src, i), part(dst, i), 3 * k + i)
+
+    def arrived_part(src, dst, k, i):
+        arrived(part(src, i), part(dst, i), 3 * k + i)
 
     def arrived_half(src, dst, k, half):
-        for part in ((0, 1), (2,))[half]:
-            arrived_part(src, dst, k, part)
+        for i in ((0, 1), (2,))[half]:
+            arrived_part(src, dst, k, i)
 
     def channels(ref, side, p, q, to):
-        block = ref[q, :, p, 16 * side : 16 * side + 16, :].astype(F32)
+        block = ref[p, :, q, 16 * side : 16 * side + 16, :].astype(F32)
         block = block.reshape(PARTS, 2, ROWS, W)
         for e in range(2):
             to[2 * p + e, :, q * W : (q + 1) * W] = block[:, e].reshape(TOK, W).astype(BF16)
@@ -242,7 +244,7 @@
     def put(dst, side, p, both):
         both = jnp.concatenate([m.reshape(PARTS, ROWS, TOK) for m in both], axis=1).astype(BF16)
         for q in range(CHUNKS):
-            dst[p, :, q, 16 * side : 16 * side + 16, :] = both[:, :, q * W : (q + 1) * W]
+            dst[q, :, p, 16 * side : 16 * side + 16, :] = both[:, :, q * W : (q + 1) * W]
 
     for q in range(CHUNKS):
 
@@ -269,14 +271,12 @@
 
     def forward_triangle(u, k):
         src, dst = (s2.at[u], r2.at[u]), (t1.at[u], u1.at[u])
-        arrived_part(*src, k - 1, 0)
         for p in range(2):
-            for side in range(2):
-                channels(src[1], side, p, 0, tri.at[u, side])
-        for p in range(2):
-            arrived_part(*src, k - 1, 1 + p)
-            for side in range(2):
-                channels(src[1], side, p, 1, tri.at[u, side])
+            for q in range(CHUNKS):
+                if (p, q) != (1, 1):
+                    arrived_part(*src, k - 1, 2 * p + q)
+                for side in range(2):
+                    channels(src[1], side, p, q, tri.at[u, side])
             both = [
                 dot(tri[u, 0, 2 * p + e], tri[u, 1, 2 * p + e], 1 - u, 1 - u) for e in range(2)
             ]
@@ -285,12 +285,11 @@
 
     def backward_triangle(u, k):
         src, dst = (s1.at[u], r1.at[u]), (t2.at[u], u2.at[u])
-        arrived_part(*src, k - 1, 0)
         for p in range(2):
-            channels(src[1], 0, p, 0, tri.at[2, 0])
-        for p in range(2):
-            arrived_part(*src, k - 1, 1 + p)
-            channels(src[1], 0, p, 1, tri.at[2, 0])
+            for q in range(CHUNKS):
+                if (p, q) != (1, 1):
+                    arrived_part(*src, k - 1, 2 * p + q)
+                channels(src[1], 0, p, q, tri.at[2, 0])
             grad = [tri[2, 0, 2 * p + e] for e in range(2)]
             left = [tri[u, 0, 2 * p + e] for e in range(2)]
             right = [tri[u, 1, 2 * p + e] for e in range(2)]
@@ -385,14 +384,13 @@
     def send_all(src, dst, k):
         dst[me] = src[...]
 
-        def go(s, _):
+        def go(t):
             pltpu.make_async_remote_copy(
                 src_ref=src, dst_ref=dst.at[me], send_sem=ssem.at[k], recv_sem=rsem.at[k],
-                device_id={"axial": partner(me, s)}, device_id_type=MESH,
+                device_id={"axial": t}, device_id_type=MESH,
             ).start()
-            return 0
-
-        lax.fori_loop(0, PARTS - 1, go, 0)
+
+        each_partner(me, go)
 
     early = [
         dot(nrm[1], gm[1], 1, 1),
@@ -424,9 +422,11 @@
         if q == 0:
             rows(functools.partial(fifth, q))
             store(q).start()
+            cells = ROWS * W
+            share[...] = dot(nrm[0, :, :cells], gm[0, : 4 * C, :cells], 1, 1)
 
     scale = 1.0 / math.sqrt(DEPTH * TOK * TOK)
-    pieces(ls, dot(nrm[0], gm[0, : 4 * C, :], 1, 1))
+    pieces(ls, share[...] + dot(nrm[0, :, cells:], gm[0, : 4 * C, cells:], 1, 1))
     send(ls, lr, last + 3)
     rows(functools.partial(fifth, 1))
     store(1).start()
@@ -529,6 +529,7 @@
             for shape in ((PARTS,), (PARTS,), (), (DEPTH,), (), (PARTS,))
         ]
         + [
+            pltpu.VMEM((C, 4 * C), F32),
             pltpu.SemaphoreType.DMA((8 * 3 + 6,)),
             pltpu.SemaphoreType.DMA((8 * 3 + 6,)),
             pltpu.SemaphoreType.DMA((10,)),

time: 136 us -> 130 us (0.956)
  Pallas kernels: 134 us -> 128 us
    pallas_call x1, Pallas kernels: 131 us -> 125 us  [body(): pl.pallas_call(kernel, out_shape=[jax.ShapeDtypeStruct((ROWS, TOK, C), F3...]
where the time goes in v3:
time: 130 us
  Pallas kernels  128 us (98%)
  between operations  1.3 us (1%)
    pallas_call x1, Pallas kernels, body(): pl.pallas_call(kernel, out_shape=[jax.ShapeDtypeStruct((ROWS, TOK, C), F3...  125 us
    pallas_call x1, Pallas kernels, body(): pl.pallas_call(finish, out_shape=[jax.ShapeDtypeStruct((ROWS, TOK, C), F3...  2.97 us

profile of v3, /device:TPU:1, one launch (start us, length us, event | category | flops | bytes accessed | tf_op | source)
XLA Modules:
  0.0 129.5 jit_solution(1690431944794252429)
XLA Ops:
  1.3 125.3 %shard_map.178 = (f32[8,256,128]{2,1,0:T(8,128)}, bf16[32,16,256]{2,1,0:T(8,128)(2,1)}, bf16[32,16,128]{2,1,0:T(8,128)(2,1)}) custom-call(s32[1]{0:T(128)S(6)} %copy.20.len_ref, bf16[8,256,128]{2,1,0:T(8,128)(2,1)} %bitcast.11, bf16[8,256,128]{2,1,0:T(8,128)(2,1)} %bitcast.12, f32[1,128]{1,0:T(1,128)} %bitcast.13, f32[128,640]{1,0:T(8,128)} %p1.1, ...), custom_call_target="tpu_custom_call" | custom-call | tf_op jit(solution)/shard_map/pallas_call | solution.py:482
  126.6 3.0 %shard_map.179 = (f32[8,256,128]{2,1,0:T(8,128)}, f32[1,128]{1,0:T(1,128)}, f32[128,640]{1,0:T(8,128)}, f32[1,128]{1,0:T(1,128)}, f32[128,128]{1,0:T(8,128)}, /*...) custom-call(f32[8,256,128]{2,1,0:T(8,128)} %get-tuple-element.21.big, ...), custom_call_target="tpu_custom_call" | custom-call | tf_op jit(solution)/shard_map/pallas_call | solution.py:542

commit v4 on v3

--- a/solution.py
+++ b/solution.py
@@ -157,7 +157,10 @@
             st[u, b, side * C : (side + 1) * C, :] = value
             st[u, b, (2 + side) * C : (3 + side) * C, :] = sig
             tmp[side, strided(r), :] = value * sig * mask
-        st[u, b, 4 * C :, :] = sigmoid(dot(pjt[u, 4 * C :, :], normed))
+
+    def output_gate(u, q, r):
+        normed = nrm[u, :, cut(q, r)]
+        st[u, q * ROWS + r, 4 * C :, :] = sigmoid(dot(pjt[u, 4 * C :, :], normed))
 
     def leave(u, q, r):
         b = q * ROWS + r
@@ -266,6 +269,7 @@
 
         def turn(r):
             ct[q * ROWS + r] = cot_ref[r, q * W : (q + 1) * W, :].astype(F32).T
+            output_gate(0, q, r)
 
         rows(turn)
 
@@ -318,6 +322,9 @@
         rows(second)
         pack(s2.at[1], q, 2)
         send_chunk(s2.at[1], r2.at[1], 2, q)
+
+    for q in range(CHUNKS):
+        rows(functools.partial(output_gate, 1, q))
 
     forward_triangle(1, 3)
 

time: 130 us -> 130 us (level)
  no operation moved by 1% of the time
where the time goes in v4:
time: 130 us
  Pallas kernels  129 us (99%)
  between operations  1.3 us (1%)
    pallas_call x1, Pallas kernels, body(): pl.pallas_call(kernel, out_shape=[jax.ShapeDtypeStruct((ROWS, TOK, C), F3...  126 us
    pallas_call x1, Pallas kernels, body(): pl.pallas_call(finish, out_shape=[jax.ShapeDtypeStruct((ROWS, TOK, C), F3...  2.97 us

profile of v4, /device:TPU:1, one launch (start us, length us, event | category | flops | bytes accessed | tf_op | source)
XLA Modules:
  0.0 130.0 jit_solution(18390645471700326603)
XLA Ops:
  1.3 125.8 %shard_map.178 = (f32[8,256,128]{2,1,0:T(8,128)}, bf16[32,16,256]{2,1,0:T(8,128)(2,1)}, bf16[32,16,128]{2,1,0:T(8,128)(2,1)}) custom-call(s32[1]{0:T(128)S(6)} %copy.20.len_ref, bf16[8,256,128]{2,1,0:T(8,128)(2,1)} %bitcast.11, bf16[8,256,128]{2,1,0:T(8,128)(2,1)} %bitcast.12, f32[1,128]{1,0:T(1,128)} %bitcast.13, f32[128,640]{1,0:T(8,128)} %p1.1, ...), custom_call_target="tpu_custom_call" | custom-call | tf_op jit(solution)/shard_map/pallas_call | solution.py:489
  127.1 3.0 %shard_map.179 = (f32[8,256,128]{2,1,0:T(8,128)}, f32[1,128]{1,0:T(1,128)}, f32[128,640]{1,0:T(8,128)}, f32[1,128]{1,0:T(1,128)}, f32[128,128]{1,0:T(8,128)}, /*...) custom-call(f32[8,256,128]{2,1,0:T(8,128)} %get-tuple-element.21.big, ...), custom_call_target="tpu_custom_call" | custom-call | tf_op jit(solution)/shard_map/pallas_call | solution.py:549
